TPU v7x, 32 devices: a whole 2x2x4 slice. The times are simulated.
32 devices in a mesh: group: 2 (over y), tx: 16 (over z, x, core).
Axes of the slice: x: 2, y: 2, z: 4, core: 2. Of those that a mesh axis runs over, the one named last changes fastest.
Arguments:
- pressure: float32 [32, 6, 8, 1024], P(('group', 'tx')), parts along dimension 0, may hold values from -4 to 4
- pressure_old: float32 [32, 6, 8, 1024], P(('group', 'tx')), parts along dimension 0, may hold values from -4 to 4
- soil_class: int32 [16, 6, 8, 1024], P('tx'), may hold values from 0 to 11
- elevation: float32 [16, 6, 1024], P('tx'), may hold values from -3 to 3
- land_mask: int32 [16, 6, 1024], P('tx'), may hold values 0 or 1
- rainfall: float32 [32, 6, 1024], P(('group', 'tx')), parts along dimension 0, may hold values from 0.1 to 1
- tile_list: int32 [16, 6], P('tx'), may hold values from -1 to 7, as said below
- neighbors: int32 [16, 6, 4], P('tx'), may hold values from -1 to 5, as said below
- atm_map: int32 [16, 6, 4], P('tx'), may hold values from -1 to 63, as said below
- forcing: float32 [2, 128, 256], P(None, ('group', 'tx')), parts along dimension 1, may hold values from 0.2 to 2
Outputs:
- pressure_new: float32 [32, 6, 8, 1024], P(('group', 'tx')), parts along dimension 0
- surface_return: float32 [32, 6, 4, 256], P(('group', 'tx')), parts along dimension 0
There are 2 independent parts, one for each index of `group`. A program takes and returns all parts, laid end to end along the dimension named above; an argument that names none is the same for every part. Nothing has to cross between parts.
Inputs may be any that keep to these rules, and one draw needn't show every extreme that they name: `tile_list`: each tile row holds distinct tile columns in random slots; every tile row holds at least half of 6 tiles (and at least 2), and some tile row in every draw fills all 6 slots. `neighbors`: west and east name slots of the same tile row, north of tile row r-1, south of tile row r+1; -1 where the neighbouring tile column is empty, outside the domain, or the slot itself is empty. `atm_map`: atmosphere row a lives on index a // 4 of tx; the rows of one tile row that go to one index of tx all go to the same atmosphere row, and there are exactly 2 of them or none; -1 exactly for empty slots.
All inputs are finite; a program needn't handle non-finite values. No bound on the sum of `land_mask` on one device may be relied on, other than what follows from the above.
Results may differ from a plain program's by a relative error of at most 0.000067.
Values sent between devices are 32-bit elements; how exact they have to be, the bound alone decides.
A program may use at most 832 MiB of HBM per device.

v0:
```python
import functools

import jax
import jax.numpy as jnp
import numpy as np
from jax import lax
from jax.experimental import pallas as pl
from jax.experimental.pallas import tpu as pltpu
from jax.sharding import PartitionSpec as P

TS = 32
ITERS = 4
LANES = 128
HALO = 2 * ITERS * TS
STRIDE = 16

KSAT = np.array(
    [0.4, 0.32, 0.26, 0.21, 0.17, 0.14, 0.115, 0.095, 0.08, 0.067, 0.057, 0.05], np.float32
)
SHAPE = np.array([3.0, 2.6, 2.2, 1.9, 1.6, 1.4, 1.2, 1.0, 0.9, 0.8, 0.7, 0.6], np.float32)
POROSITY = np.array(
    [0.38, 0.39, 0.4, 0.43, 0.45, 0.41, 0.39, 0.43, 0.44, 0.38, 0.46, 0.48], np.float32
)
LAYER_DROP = 0.25
COUPLING = 0.5
MESH = pl.DeviceIdType.MESH


def sigmoid(v):
    return 1.0 / (1.0 + jnp.exp(-v))


def kernel(
    n,
    p_in,
    old_in,
    soil_in,
    elev_in,
    land_in,
    rain_in,
    tab_in,
    own_tab,
    forcing,
    p_out,
    ret_out,
    h,
    cst,
    soil,
    elev,
    land,
    rain,
    elev_rows,
    land_rows,
    rain_rows,
    north_vec,
    south_vec,
    north_tab,
    south_tab,
    kk,
    kp,
    hh,
    step,
    qq,
    wi,
    sat,
    alpha,
    poro,
    wet,
    kf_w,
    kf_e,
    kf_n,
    kf_s,
    kf_u,
    g_w,
    g_e,
    g_n,
    g_s,
    g_u,
    flux,
    rows,
    snd,
    rcv,
    snd2,
    rcv2,
    local_sem,
    send_sem,
    recv_sem,
    tab_sem,
    a_send,
    a_recv,
    b_send,
    b_recv,
    out_sem,
):
    me = lax.axis_index("tx")
    group = lax.axis_index("group")
    slots, layers = h.shape[0], h.shape[1]
    cells = p_in.shape[-1]
    own = pl.ds(HALO, cells)
    top_part, low_part = pl.ds(0, HALO), pl.ds(HALO + cells, HALO)
    atm = forcing.shape[1]
    hc = HALO // LANES
    nq = (cells + 2 * HALO) // LANES

    big = [(p_in, h), (old_in, cst), (soil_in, soil)]
    small = [(elev_in, elev), (land_in, land), (rain_in, rain)]
    local = []
    for src, dst in big:
        local.append((src.at[0], dst.at[:, :, own]))
    for src, dst in small:
        local.append((src.at[0], dst.at[:, own]))
    locals_ = [
        pltpu.make_async_copy(src, dst, local_sem.at[i]) for i, (src, dst) in enumerate(local)
    ]
    for copy in locals_:
        copy.start()

    for part in (top_part, low_part):
        for _, dst in big:
            dst[:, :, part] = jnp.zeros((slots, layers, HALO), dst.dtype)
        for _, dst in small:
            dst[:, part] = jnp.zeros((slots, HALO), dst.dtype)
    north_vec[...] = jnp.zeros(north_vec.shape, jnp.int32)
    south_vec[...] = jnp.zeros(south_vec.shape, jnp.int32)

    barrier = pltpu.get_barrier_semaphore()

    def greet(o, carry):
        pl.semaphore_signal(
            barrier, inc=1, device_id=(group, lax.rem(me + o, n)), device_id_type=MESH
        )
        return carry

    lax.fori_loop(1, n, greet, 0)
    pl.semaphore_wait(barrier, n - 1)

    def halo_copies(way):
        src_part = pl.ds(cells - HALO, HALO) if way == 0 else pl.ds(0, HALO)
        dst_part = top_part if way == 0 else low_part
        pairs = [(tab_in, north_vec if way == 0 else south_vec)]
        pairs += [(src.at[0, :, src_part], dst.at[:, dst_part]) for src, dst in small]
        pairs += [(src.at[0, :, :, src_part], dst.at[:, :, dst_part]) for src, dst in big]
        target = me + 1 if way == 0 else me - 1
        return [
            pltpu.make_async_remote_copy(
                src_ref=src,
                dst_ref=dst,
                send_sem=send_sem.at[way, i],
                recv_sem=recv_sem.at[way, i],
                device_id=(group, target),
                device_id_type=MESH,
            )
            for i, (src, dst) in enumerate(pairs)
        ]

    @pl.when(me < n - 1)
    def _():
        for copy in halo_copies(0):
            copy.start()

    @pl.when(me > 0)
    def _():
        for copy in halo_copies(1):
            copy.start()

    for copy in locals_:
        copy.wait()

    @pl.when(me > 0)
    def _():
        for copy in halo_copies(0):
            copy.wait_recv()

    @pl.when(me < n - 1)
    def _():
        for copy in halo_copies(1):
            copy.wait_recv()

    tabs = [
        pltpu.make_async_copy(north_vec, north_tab, tab_sem.at[0]),
        pltpu.make_async_copy(south_vec, south_tab, tab_sem.at[1]),
    ]
    for copy in tabs:
        copy.start()
    for copy in tabs:
        copy.wait()

    lane = lax.broadcasted_iota(jnp.int32, (layers, LANES), 1)
    layer = lax.broadcasted_iota(jnp.int32, (layers, LANES), 0)
    x_place = lax.rem(lane, TS)
    at_west, at_east = x_place == 0, x_place == TS - 1
    at_north, at_south = lane < TS, lane >= LANES - TS
    depth = layer.astype(jnp.float32) * LAYER_DROP
    upper = jnp.where(layer > 0, 2.0, 0.0)

    def table_of(q):
        return north_tab if q < hc else (own_tab if q < nq - hc else south_tab)

    def at(q):
        return pl.ds(q * LANES, LANES)

    def entry(q, s, f):
        return table_of(q)[0, s * STRIDE + f]

    def picks(s, first, last):
        found = {}
        for sec, q in ((0, 0), (1, hc), (2, nq - hc)):
            side = []
            for f in range(4):
                number = entry(q, s, f)
                side.append((jnp.maximum(number, 0), jnp.where(number >= 0, 1.0, 0.0)))
            found[sec] = side
        return found

    def section(q):
        return 0 if q < hc else (1 if q < nq - hc else 2)

    def around(field, s, q, found):
        side = found[section(q)]
        mid = field[s, :, at(q)]
        west = jnp.where(
            at_west,
            pltpu.roll(field[side[0][0], :, at(q)], LANES - TS + 1, 1),
            pltpu.roll(mid, 1, 1),
        )
        east = jnp.where(
            at_east,
            pltpu.roll(field[side[1][0], :, at(q)], TS - 1, 1),
            pltpu.roll(mid, LANES - 1, 1),
        )
        north_slot = side[2][0] if q in (hc, nq - hc) else s
        south_slot = side[3][0] if q in (hc - 1, nq - hc - 1) else s
        above = field[north_slot, :, at(max(q - 1, 0))]
        below = field[south_slot, :, at(min(q + 1, nq - 1))]
        north = pltpu.roll(jnp.where(at_south, above, mid), TS, 1)
        south = pltpu.roll(jnp.where(at_north, below, mid), LANES - TS, 1)
        return mid, west, east, north, south

    def conductivity(s, q, head):
        relative = sigmoid(2.0 * head)
        conduct = sat[s, :, at(q)] * relative
        kk[s, :, at(q)] = conduct
        kp[s, :, at(q)] = 2.0 * conduct * (1.0 - relative)

    def prepare(s, carry):
        for q in range(nq):
            classes = soil[s, :, at(q)]
            tables = [jnp.full((layers, LANES), float(t[0]), jnp.float32) for t in (KSAT, SHAPE, POROSITY)]
            for number in range(1, KSAT.shape[0]):
                hit = classes == number
                tables = [
                    jnp.where(hit, float(t[number]), v)
                    for t, v in zip((KSAT, SHAPE, POROSITY), tables)
                ]
            sat[s, :, at(q)] = 0.5 * tables[0]
            alpha[s, :, at(q)] = tables[1]
            poro[s, :, at(q)] = tables[2]
            old = cst[s, :, at(q)]
            rain_top = jnp.where(layer == 0, rain_rows[s, :, at(q)], 0.0)
            cst[s, :, at(q)] = 0.25 * (old + tables[2] * sigmoid(tables[1] * old)) + rain_top
            held = jnp.where(entry(q, s, 4) >= 0, 1.0, 0.0)
            wet[s, :, at(q)] = jnp.broadcast_to(
                jnp.where(land_rows[s, :, at(q)] > 0, held, 0.0), (layers, LANES)
            )
            head = h[s, :, at(q)]
            hh[s, :, at(q)] = head + (elev_rows[s, :, at(q)] - depth)
            conductivity(s, q, head)
        return carry

    for s in range(slots):
        for source, spread_rows in ((elev, elev_rows), (land, land_rows), (rain, rain_rows)):
            spread_rows[s] = source[s : s + 1, :]
    lax.fori_loop(0, slots, prepare, 0)

    def balance(first, last, s, carry):
        found = picks(s, first, last)
        for q in range(first, last):
            side = found[section(q)]
            k0, k_w, k_e, k_n, k_s = around(kk, s, q, found)
            h0, h_w, h_e, h_n, h_s = around(hh, s, q, found)
            mask_w = jnp.where(at_west, side[0][1], 1.0)
            mask_e = jnp.where(at_east, side[1][1], 1.0)
            mask_n = mask_s = None
            if q in (hc, nq - hc):
                mask_n = jnp.where(at_north, side[2][1], 1.0)
            if q == 0:
                mask_n = jnp.where(at_north, 0.0, 1.0)
            if q in (hc - 1, nq - hc - 1):
                mask_s = jnp.where(at_south, side[3][1], 1.0)
            if q == nq - 1:
                mask_s = jnp.where(at_south, 0.0, 1.0)
            inflow = None
            for k_j, h_j, mask, k_ref, g_ref in (
                (k_w, h_w, mask_w, kf_w, g_w),
                (k_e, h_e, mask_e, kf_e, g_e),
                (k_n, h_n, mask_n, kf_n, g_n),
                (k_s, h_s, mask_s, kf_s, g_s),
            ):
                face, drop = k0 + k_j, h_j - h0
                weighted = drop
                if mask is not None:
                    face, weighted = face * mask, drop * mask
                k_ref[s, :, at(q)] = face
                g_ref[s, :, at(q)] = weighted
                flow = face * drop
                inflow = flow if inflow is None else inflow + flow
                total = face if k_ref is kf_w else total + face
            drop = pltpu.roll(h0, 1, 0) - h0
            face = (k0 + pltpu.roll(k0, 1, 0)) * upper
            kf_u[s, :, at(q)] = face
            g_u[s, :, at(q)] = drop * upper
            flow = face * drop
            inflow = inflow + flow - pltpu.roll(flow, layers - 1, 0)
            total = total + face + pltpu.roll(face, layers - 1, 0)
            head = h[s, :, at(q)]
            shape = alpha[s, :, at(q)]
            pore = poro[s, :, at(q)]
            theta = sigmoid(shape * head)
            storage = 0.25 * (1.0 + pore * shape * theta * (1.0 - theta))
            residual = 0.25 * (head + pore * theta) - cst[s, :, at(q)] - inflow
            scaled = wet[s, :, at(q)] / (storage + total)
            move = scaled * residual
            wi[s, :, at(q)] = scaled
            step[s, :, at(q)] = move
            qq[s, :, at(q)] = kp[s, :, at(q)] * move
        return carry

    def advance(first, last, final, s, carry):
        found = picks(s, first, last)
        for q in range(first, last):
            s0, s_w, s_e, s_n, s_s = around(step, s, q, found)
            q0, q_w, q_e, q_n, q_s = around(qq, s, q, found)
            gsum = acc = None
            for s_j, q_j, k_ref, g_ref in (
                (s_w, q_w, kf_w, g_w),
                (s_e, q_e, kf_e, g_e),
                (s_n, q_n, kf_n, g_n),
                (s_s, q_s, kf_s, g_s),
            ):
                grad = g_ref[s, :, at(q)]
                term = k_ref[s, :, at(q)] * s_j + grad * q_j
                acc = term if acc is None else acc + term
                gsum = grad if gsum is None else gsum + grad
            face, grad = kf_u[s, :, at(q)], g_u[s, :, at(q)]
            acc = acc + face * pltpu.roll(s0, 1, 0) + grad * pltpu.roll(q0, 1, 0)
            acc = acc + pltpu.roll(face * s0 - grad * q0, layers - 1, 0)
            gsum = gsum + grad - pltpu.roll(grad, layers - 1, 0)
            change = s0 + wi[s, :, at(q)] * (acc + q0 * gsum)
            head = h[s, :, at(q)] - change
            h[s, :, at(q)] = head
            if final:
                strength = 2.0 * wet[s, :, at(q)] * sat[s, :, at(q)] * sigmoid(2.0 * head)
                half, part = divmod(q - hc, HALO // LANES)
                flux[s * 4 + half, :, pl.ds(part * LANES, LANES)] = strength[0:1]
            else:
                hh[s, :, at(q)] = hh[s, :, at(q)] - change
                conductivity(s, q, head)
        return carry

    rows_per = LANES // TS
    for number in range(ITERS):
        rows_a = 2 * ITERS - 1 - 2 * number
        rows_b = rows_a - 1
        wide_a, wide_b = -(-rows_a // rows_per), -(-rows_b // rows_per)
        lax.fori_loop(
            0, slots, functools.partial(balance, hc - wide_a, nq - hc + wide_a), 0
        )
        lax.fori_loop(
            0,
            slots,
            functools.partial(advance, hc - wide_b, nq - hc + wide_b, number == ITERS - 1),
            0,
        )

    quarter = flux.shape[-1]
    place = lax.broadcasted_iota(jnp.int32, (n, LANES), 0) * atm
    wide_place = lax.broadcasted_iota(jnp.int32, (n, quarter), 0) * atm

    def collect(s, carry):
        sums, label = carry
        for k in range(4):
            number = own_tab[0, s * STRIDE + 5 + k]
            there = number - wide_place
            hit = (there >= 0) & (there < atm)
            sums = sums + jnp.where(hit, flux[s * 4 + k], 0.0)
            there = number - place
            hit = (there >= 0) & (there < atm)
            label = jnp.where(hit, (there + 1).astype(jnp.float32), label)
        return sums, label

    sums, label = lax.fori_loop(
        0,
        slots,
        collect,
        (jnp.zeros((n, quarter), jnp.float32), jnp.zeros((n, LANES), jnp.float32)),
    )
    for d in range(n):
        snd[d, :, pl.ds(0, quarter)] = sums[d : d + 1]
        snd[d, :, pl.ds(quarter, LANES)] = label[d : d + 1]

    def exchange(src, dst, s_sem, r_sem):
        def one(o):
            peer = lax.rem(me + o, n)
            return pltpu.make_async_remote_copy(
                src_ref=src.at[peer],
                dst_ref=dst.at[me],
                send_sem=s_sem.at[o],
                recv_sem=r_sem.at[o],
                device_id=(group, peer),
                device_id_type=MESH,
            )

        def begin(o, carry):
            one(o).start()
            return carry

        def take(o, carry):
            source = lax.rem(me - o + n, n)
            pltpu.make_async_remote_copy(
                src_ref=src.at[source],
                dst_ref=dst.at[source],
                send_sem=s_sem.at[o],
                recv_sem=r_sem.at[o],
                device_id=(group, source),
                device_id_type=MESH,
            ).wait_recv()
            return carry

        def end(o, carry):
            one(o).wait_send()
            return carry

        lax.fori_loop(1, n, begin, 0)
        dst[me] = src[me]
        lax.fori_loop(1, n, take, 0)
        return lambda: lax.fori_loop(1, n, end, 0)

    finish_a = exchange(snd, rcv, a_send, a_recv)

    for d in range(n):
        rows[d : d + 1, :] = rcv[d]
    got = rows[:, pl.ds(0, quarter)]
    tag = rows[:, pl.ds(quarter, LANES)]
    tag = jnp.concatenate([tag] * (quarter // LANES), axis=1)

    back = jnp.zeros((n, quarter), jnp.float32)
    for a in range(atm):
        hit = tag == float(a + 1)
        total = jnp.sum(jnp.where(hit, got, 0.0), axis=0, keepdims=True)
        count = jnp.sum(jnp.where(hit, 2.0, 0.0), axis=0, keepdims=True)
        mean = total / jnp.maximum(count, 1.0)
        demand = forcing[0, a : a + 1, :]
        supply = forcing[1, a : a + 1, :]
        rate = supply - demand * mean / (mean + demand)
        back = jnp.where(hit, rate, back)

    for d in range(n):
        snd2[d] = back[d : d + 1]
    finish_b = exchange(snd2, rcv2, b_send, b_recv)

    def settle(s, carry):
        for k in range(4):
            number = own_tab[0, s * STRIDE + 5 + k]
            live = jnp.where(number >= 0, 1.0, 0.0)
            rate = rcv2[lax.div(jnp.maximum(number, 0), atm)] * live
            ret_out[0, s, pl.ds(k, 1), :] = rate
            for part in range(quarter // LANES):
                q = hc + k * (quarter // LANES) + part
                piece = rate[:, part * LANES : (part + 1) * LANES]
                h[s, :, at(q)] = h[s, :, at(q)] + jnp.where(
                    layer == 0, COUPLING * wet[s, :, at(q)] * piece, 0.0
                )
        return carry

    lax.fori_loop(0, slots, settle, 0)
    out = pltpu.make_async_copy(h.at[:, :, own], p_out.at[0], out_sem)
    out.start()
    finish_a()
    finish_b()

    @pl.when(me < n - 1)
    def _():
        for copy in halo_copies(0):
            copy.wait_send()

    @pl.when(me > 0)
    def _():
        for copy in halo_copies(1):
            copy.wait_send()

    out.wait()


def on_device(n, *args):
    (pressure, pressure_old, soil, elev, land, rain, tiles, neighbors, atm_map, forcing) = args
    _, slots, layers, cells = pressure.shape
    quarter = cells // 4
    wide = cells + 2 * HALO
    table = jnp.concatenate([neighbors[0], tiles[0][:, None], atm_map[0]], axis=1)
    table = jnp.pad(table, ((0, 0), (0, STRIDE - table.shape[1]))).reshape(1, slots * STRIDE)
    table = jnp.pad(table, ((0, 0), (0, -table.shape[1] % LANES)))
    width = table.shape[1]
    vec, smem, anywhere = pltpu.VMEM, pltpu.SMEM, pl.ANY

    def cube(kind=jnp.float32):
        return vec((slots, layers, wide), kind)

    def flat(kind=jnp.float32):
        return vec((slots, wide), kind)

    def lines(kind=jnp.float32):
        return vec((slots, 1, wide), kind)

    dma = pltpu.SemaphoreType.DMA
    return tuple(pl.pallas_call(
        functools.partial(kernel, n),
        out_shape=[
            jax.ShapeDtypeStruct(pressure.shape, jnp.float32),
            jax.ShapeDtypeStruct((1, slots, 4, quarter), jnp.float32),
        ],
        in_specs=[pl.BlockSpec(memory_space=anywhere)] * 7
        + [pl.BlockSpec(memory_space=smem), pl.BlockSpec(memory_space=vec)],
        out_specs=[pl.BlockSpec(memory_space=anywhere), pl.BlockSpec(memory_space=vec)],
        scratch_shapes=[
            cube(),
            cube(),
            cube(jnp.int32),
            flat(),
            flat(jnp.int32),
            flat(),
            lines(),
            lines(jnp.int32),
            lines(),
            vec((1, width), jnp.int32),
            vec((1, width), jnp.int32),
            smem((1, width), jnp.int32),
            smem((1, width), jnp.int32),
        ]
        + [cube()] * 20
        + [
            vec((slots * 4, 1, quarter), jnp.float32),
            vec((n, quarter + LANES), jnp.float32),
            vec((n, 1, quarter + LANES), jnp.float32),
            vec((n, 1, quarter + LANES), jnp.float32),
            vec((n, 1, quarter), jnp.float32),
            vec((n, 1, quarter), jnp.float32),
            dma((6,)),
            dma((2, 7)),
            dma((2, 7)),
            dma((2,)),
            dma((n,)),
            dma((n,)),
            dma((n,)),
            dma((n,)),
            dma,
        ],
        compiler_params=pltpu.CompilerParams(
            collective_id=0, has_side_effects=True, vmem_limit_bytes=60 * 2**20
        ),
    )(pressure, pressure_old, soil, elev, land, rain, table, table, forcing))


def solution(mesh):
    both = ("group", "tx")
    in_specs = (
        P(both, None, None, None),
        P(both, None, None, None),
        P("tx", None, None, None),
        P("tx", None, None),
        P("tx", None, None),
        P(both, None, None),
        P("tx", None),
        P("tx", None, None),
        P("tx", None, None),
        P(None, both, None),
    )
    out_specs = [P(both, None, None, None), P(both, None, None, None)]
    return jax.shard_map(
        functools.partial(on_device, mesh.shape["tx"]),
        mesh=mesh,
        in_specs=in_specs,
        out_specs=tuple(out_specs),
        check_vma=False,
    )
```

profile of v0, /device:TPU:0, one launch (start us, length us, event | category | flops | bytes accessed | tf_op | source)
XLA Modules:
  0.0 41.3 jit_solution(6375910224675930223)
XLA Ops:
  0.6 0.0 copy-start
  0.6 0.7 %pad_add_fusion = s32[6,9]{0,1:T(8,128)S(1)} fusion(s32[6,4]{0,1:T(4,128)} %bitcast.3, s32[6,1]{0,1:T(1,128)} %bitcast.5, s32[6,4]{0,1:T(4,128)} %bitcast.4), kind=kLoop, calls=%fused_computation | loop fusion | flops 108 | bytes 432 | tf_op jit(solution)/shard_map/concatenate | solution.py:499
  1.4 0.1 copy.16
  1.5 0.1 reshape.7
  1.6 0.5 %pad.9.tab_in.own_tab = s32[1,128]{1,0:T(1,128)} pad(s32[1,96]{1,0:T(1,128)S(1)} %reshape.7, s32[]{:T(128)} %constant.0.clone.1), padding=0_0x0_32 | pad | bytes 900 | tf_op jit(solution)/shard_map/jit(_pad)/pad | solution.py:501
  2.1 0.0 copy-done
  2.1 0.0 copy-start.1
  2.1 0.6 %copy.13.elev_in = f32[1,6,1024]{2,1,0:T(8,128)} copy(f32[1,6,1024]{2,0,1:T(1,128)S(1)} %copy-done) | data formatting | bytes 49152 | tf_op args[3]
  2.7 0.1 copy-done.1
  2.8 0.0 copy-start.2
  2.8 0.6 %copy.14.land_in = s32[1,6,1024]{2,1,0:T(8,128)} copy(s32[1,6,1024]{2,0,1:T(1,128)S(1)} %copy-done.1) | data formatting | bytes 49152 | tf_op args[4]
  3.4 0.1 copy-done.2
  3.6 0.6 %copy.15.rain_in = f32[1,6,1024]{2,1,0:T(8,128)} copy(f32[1,6,1024]{2,0,1:T(1,128)S(1)} %copy-done.2) | data formatting | bytes 49152 | tf_op args[5]
  4.2 34.8 %shard_map.113 = (f32[1,6,8,1024]{3,2,1,0:T(8,128)}, f32[1,6,4,256]{3,2,1,0:T(4,128)}) custom-call(f32[1,6,8,1024]{3,2,1,0:T(8,128)} %p_in.1, f32[1,6,8,1024]{3,2,1,0:T(8,128)} %old_in.1, s32[1,6,8,1024]{3,2,1,0:T(8,128)} %soil_in.1, f32[1,6,1024]{2,1,0:T(8,128)} %copy.13.elev_in, s32[1,6,1024]{2,1,0:T(8,128)} %copy.14.land_in, f32[1,6,1024]{2,1,0:T(8,128)} %copy.15.rain_in, ...), custom_call_target="tpu_custom_call" | custom-call | tf_op jit(solution)/shard_map/pallas_call | solution.py:515
  39.0 0.0 copy-start.3
  39.0 1.6 %copy.19 = f32[1,6,8,1024]{3,2,1,0:T(8,128)} copy(f32[1,6,8,1024]{3,2,1,0:T(8,128)} %get-tuple-element.4) | data formatting | bytes 393216
  40.7 0.0 copy-done.3
  40.7 0.6 %copy.20 = f32[1,6,4,256]{3,2,1,0:T(4,128)} copy(f32[1,6,4,256]{3,2,1,0:T(4,128)S(1)} %copy-done.3) | data formatting | bytes 49152
  (1 shorter events, 0.0 us)
Async XLA Ops:
  0.6 1.4 %copy-start = (f32[1,6,1024]{2,0,1:T(1,128)S(1)}, f32[1,6,1024]{2,0,1:T(1,128)}, u32[]{:S(2)}) copy-start(f32[1,6,1024]{2,0,1:T(1,128)} %param.13) | copy-start | bytes 73732
  2.1 0.7 %copy-start.1 = (s32[1,6,1024]{2,0,1:T(1,128)S(1)}, s32[1,6,1024]{2,0,1:T(1,128)}, u32[]{:S(2)}) copy-start(s32[1,6,1024]{2,0,1:T(1,128)} %param.14) | copy-start | bytes 73732
  2.8 0.7 %copy-start.2 = (f32[1,6,1024]{2,0,1:T(1,128)S(1)}, f32[1,6,1024]{2,0,1:T(1,128)}, u32[]{:S(2)}) copy-start(f32[1,6,1024]{2,0,1:T(1,128)} %param.15) | copy-start | bytes 73732
  39.0 1.6 %copy-start.3 = (f32[1,6,4,256]{3,2,1,0:T(4,128)S(1)}, f32[1,6,4,256]{3,2,1,0:T(4,128)}, u32[]{:S(2)}) copy-start(f32[1,6,4,256]{3,2,1,0:T(4,128)} %get-tuple-element.5) | copy-start | bytes 73732
where the time goes:
time: 41.6 us; the launch traced here: 41.3 us
  Pallas kernels  34.8 us (84%)
  local copies, waits for them, and re-layouts  5.03 us (12%)
  other arithmetic  0.73 us (2%)
  between operations  0.66 us (2%)
    pallas_call x1, Pallas kernels, on_device(): pl.pallas_call(functools.partial(kernel, n), out_shape=[jax.ShapeDtypeStr...  34.8 us
    unnamed x14, local copies, waits for them, and re-layouts  4.43 us

commit v1 on v0

--- a/solution.py
+++ b/solution.py
@@ -12,7 +12,6 @@
 ITERS = 4
 LANES = 128
 HALO = 2 * ITERS * TS
-STRIDE = 16
 
 KSAT = np.array(
     [0.4, 0.32, 0.26, 0.21, 0.17, 0.14, 0.115, 0.095, 0.08, 0.067, 0.057, 0.05], np.float32
@@ -38,9 +37,10 @@
     elev_in,
     land_in,
     rain_in,
-    tab_in,
-    own_tab,
-    forcing,
+    nb_in,
+    tile_in,
+    atm_in,
+    forcing_in,
     p_out,
     ret_out,
     h,
@@ -49,13 +49,19 @@
     elev,
     land,
     rain,
-    elev_rows,
-    land_rows,
-    rain_rows,
-    north_vec,
-    south_vec,
-    north_tab,
-    south_tab,
+    north_nb_vec,
+    south_nb_vec,
+    north_tile_vec,
+    south_tile_vec,
+    north_nb,
+    south_nb,
+    north_tile,
+    south_tile,
+    own_nb,
+    own_tile,
+    own_atm,
+    forcing,
+    ret,
     kk,
     kp,
     hh,
@@ -108,7 +114,8 @@
     for src, dst in big:
         local.append((src.at[0], dst.at[:, :, own]))
     for src, dst in small:
-        local.append((src.at[0], dst.at[:, own]))
+        local.append((src, dst.at[:, :, own]))
+    local += [(nb_in, own_nb), (tile_in, own_tile), (atm_in, own_atm), (forcing_in, forcing)]
     locals_ = [
         pltpu.make_async_copy(src, dst, local_sem.at[i]) for i, (src, dst) in enumerate(local)
     ]
@@ -119,9 +126,9 @@
         for _, dst in big:
             dst[:, :, part] = jnp.zeros((slots, layers, HALO), dst.dtype)
         for _, dst in small:
-            dst[:, part] = jnp.zeros((slots, HALO), dst.dtype)
-    north_vec[...] = jnp.zeros(north_vec.shape, jnp.int32)
-    south_vec[...] = jnp.zeros(south_vec.shape, jnp.int32)
+            dst[:, :, part] = jnp.zeros((slots, 1, HALO), dst.dtype)
+    for dst in (north_nb_vec, south_nb_vec, north_tile_vec, south_tile_vec):
+        dst[...] = jnp.zeros(dst.shape, jnp.int32)
 
     barrier = pltpu.get_barrier_semaphore()
 
@@ -137,8 +144,11 @@
     def halo_copies(way):
         src_part = pl.ds(cells - HALO, HALO) if way == 0 else pl.ds(0, HALO)
         dst_part = top_part if way == 0 else low_part
-        pairs = [(tab_in, north_vec if way == 0 else south_vec)]
-        pairs += [(src.at[0, :, src_part], dst.at[:, dst_part]) for src, dst in small]
+        pairs = [
+            (nb_in, north_nb_vec if way == 0 else south_nb_vec),
+            (tile_in, north_tile_vec if way == 0 else south_tile_vec),
+        ]
+        pairs += [(src.at[:, :, src_part], dst.at[:, :, dst_part]) for src, dst in small]
         pairs += [(src.at[0, :, :, src_part], dst.at[:, :, dst_part]) for src, dst in big]
         target = me + 1 if way == 0 else me - 1
         return [
@@ -166,25 +176,6 @@
     for copy in locals_:
         copy.wait()
 
-    @pl.when(me > 0)
-    def _():
-        for copy in halo_copies(0):
-            copy.wait_recv()
-
-    @pl.when(me < n - 1)
-    def _():
-        for copy in halo_copies(1):
-            copy.wait_recv()
-
-    tabs = [
-        pltpu.make_async_copy(north_vec, north_tab, tab_sem.at[0]),
-        pltpu.make_async_copy(south_vec, south_tab, tab_sem.at[1]),
-    ]
-    for copy in tabs:
-        copy.start()
-    for copy in tabs:
-        copy.wait()
-
     lane = lax.broadcasted_iota(jnp.int32, (layers, LANES), 1)
     layer = lax.broadcasted_iota(jnp.int32, (layers, LANES), 0)
     x_place = lax.rem(lane, TS)
@@ -193,21 +184,23 @@
     depth = layer.astype(jnp.float32) * LAYER_DROP
     upper = jnp.where(layer > 0, 2.0, 0.0)
 
-    def table_of(q):
-        return north_tab if q < hc else (own_tab if q < nq - hc else south_tab)
-
     def at(q):
         return pl.ds(q * LANES, LANES)
 
-    def entry(q, s, f):
-        return table_of(q)[0, s * STRIDE + f]
+    def neighbor(q, s, f):
+        if hc <= q < nq - hc:
+            return own_nb[0, f, s]
+        return (north_nb if q < hc else south_nb)[0, f, s]
+
+    def tile(q, s):
+        return (north_tile if q < hc else (own_tile if q < nq - hc else south_tile))[0, s]
 
     def picks(s, first, last):
         found = {}
         for sec, q in ((0, 0), (1, hc), (2, nq - hc)):
             side = []
             for f in range(4):
-                number = entry(q, s, f)
+                number = neighbor(q, s, f)
                 side.append((jnp.maximum(number, 0), jnp.where(number >= 0, 1.0, 0.0)))
             found[sec] = side
         return found
@@ -242,8 +235,8 @@
         kk[s, :, at(q)] = conduct
         kp[s, :, at(q)] = 2.0 * conduct * (1.0 - relative)
 
-    def prepare(s, carry):
-        for q in range(nq):
+    def prepare(parts, s, carry):
+        for q in parts:
             classes = soil[s, :, at(q)]
             tables = [jnp.full((layers, LANES), float(t[0]), jnp.float32) for t in (KSAT, SHAPE, POROSITY)]
             for number in range(1, KSAT.shape[0]):
@@ -256,21 +249,47 @@
             alpha[s, :, at(q)] = tables[1]
             poro[s, :, at(q)] = tables[2]
             old = cst[s, :, at(q)]
-            rain_top = jnp.where(layer == 0, rain_rows[s, :, at(q)], 0.0)
+            rain_top = jnp.where(layer == 0, rain[s, :, at(q)], 0.0)
             cst[s, :, at(q)] = 0.25 * (old + tables[2] * sigmoid(tables[1] * old)) + rain_top
-            held = jnp.where(entry(q, s, 4) >= 0, 1.0, 0.0)
+            held = jnp.where(tile(q, s) >= 0, 1.0, 0.0)
             wet[s, :, at(q)] = jnp.broadcast_to(
-                jnp.where(land_rows[s, :, at(q)] > 0, held, 0.0), (layers, LANES)
+                jnp.where(land[s, :, at(q)] > 0, held, 0.0), (layers, LANES)
             )
             head = h[s, :, at(q)]
-            hh[s, :, at(q)] = head + (elev_rows[s, :, at(q)] - depth)
+            hh[s, :, at(q)] = head + (elev[s, :, at(q)] - depth)
             conductivity(s, q, head)
         return carry
 
-    for s in range(slots):
-        for source, spread_rows in ((elev, elev_rows), (land, land_rows), (rain, rain_rows)):
-            spread_rows[s] = source[s : s + 1, :]
-    lax.fori_loop(0, slots, prepare, 0)
+    lax.fori_loop(0, slots, functools.partial(prepare, range(hc, nq - hc)), 0)
+
+    @pl.when(me > 0)
+    def _():
+        for copy in halo_copies(0):
+            copy.wait_recv()
+
+    @pl.when(me < n - 1)
+    def _():
+        for copy in halo_copies(1):
+            copy.wait_recv()
+
+    tabs = [
+        pltpu.make_async_copy(src, dst, tab_sem.at[i])
+        for i, (src, dst) in enumerate(
+            (
+                (north_nb_vec, north_nb),
+                (south_nb_vec, south_nb),
+                (north_tile_vec, north_tile),
+                (south_tile_vec, south_tile),
+            )
+        )
+    ]
+    for copy in tabs:
+        copy.start()
+    for copy in tabs:
+        copy.wait()
+
+    halo_parts = tuple(range(hc)) + tuple(range(nq - hc, nq))
+    lax.fori_loop(0, slots, functools.partial(prepare, halo_parts), 0)
 
     def balance(first, last, s, carry):
         found = picks(s, first, last)
@@ -379,7 +398,7 @@
     def collect(s, carry):
         sums, label = carry
         for k in range(4):
-            number = own_tab[0, s * STRIDE + 5 + k]
+            number = own_atm[0, k, s]
             there = number - wide_place
             hit = (there >= 0) & (there < atm)
             sums = sums + jnp.where(hit, flux[s * 4 + k], 0.0)
@@ -404,8 +423,8 @@
             return pltpu.make_async_remote_copy(
                 src_ref=src.at[peer],
                 dst_ref=dst.at[me],
-                send_sem=s_sem.at[o],
-                recv_sem=r_sem.at[o],
+                send_sem=s_sem,
+                recv_sem=r_sem,
                 device_id=(group, peer),
                 device_id_type=MESH,
             )
@@ -414,26 +433,15 @@
             one(o).start()
             return carry
 
-        def take(o, carry):
-            source = lax.rem(me - o + n, n)
-            pltpu.make_async_remote_copy(
-                src_ref=src.at[source],
-                dst_ref=dst.at[source],
-                send_sem=s_sem.at[o],
-                recv_sem=r_sem.at[o],
-                device_id=(group, source),
-                device_id_type=MESH,
-            ).wait_recv()
-            return carry
-
-        def end(o, carry):
-            one(o).wait_send()
-            return carry
-
         lax.fori_loop(1, n, begin, 0)
         dst[me] = src[me]
-        lax.fori_loop(1, n, take, 0)
-        return lambda: lax.fori_loop(1, n, end, 0)
+        everyone = pltpu.make_async_copy(
+            src.at[pl.ds(0, n - 1)], dst.at[pl.ds(0, n - 1)], r_sem
+        )
+        everyone.wait()
+        return lambda: pltpu.make_async_copy(
+            src.at[pl.ds(0, n - 1)], dst.at[pl.ds(0, n - 1)], s_sem
+        ).wait()
 
     finish_a = exchange(snd, rcv, a_send, a_recv)
 
@@ -460,10 +468,10 @@
 
     def settle(s, carry):
         for k in range(4):
-            number = own_tab[0, s * STRIDE + 5 + k]
+            number = own_atm[0, k, s]
             live = jnp.where(number >= 0, 1.0, 0.0)
             rate = rcv2[lax.div(jnp.maximum(number, 0), atm)] * live
-            ret_out[0, s, pl.ds(k, 1), :] = rate
+            ret[0, s, pl.ds(k, 1), :] = rate
             for part in range(quarter // LANES):
                 q = hc + k * (quarter // LANES) + part
                 piece = rate[:, part * LANES : (part + 1) * LANES]
@@ -473,8 +481,12 @@
         return carry
 
     lax.fori_loop(0, slots, settle, 0)
-    out = pltpu.make_async_copy(h.at[:, :, own], p_out.at[0], out_sem)
-    out.start()
+    outs = [
+        pltpu.make_async_copy(h.at[:, :, own], p_out.at[0], out_sem.at[0]),
+        pltpu.make_async_copy(ret, ret_out, out_sem.at[1]),
+    ]
+    for copy in outs:
+        copy.start()
     finish_a()
     finish_b()
 
@@ -488,7 +500,31 @@
         for copy in halo_copies(1):
             copy.wait_send()
 
-    out.wait()
+    for copy in outs:
+        copy.wait()
+
+
+def copy_kernel(*refs):
+    count = len(refs) // 2
+    sems = refs[-1]
+    copies = [
+        pltpu.make_async_copy(refs[i], refs[count + i], sems.at[i]) for i in range(count)
+    ]
+    for copy in copies:
+        copy.start()
+    for copy in copies:
+        copy.wait()
+
+
+def hand_over(arrays):
+    return pl.pallas_call(
+        copy_kernel,
+        out_shape=[jax.ShapeDtypeStruct(v.shape, v.dtype) for v in arrays],
+        in_specs=[pl.BlockSpec(memory_space=pl.ANY)] * len(arrays),
+        out_specs=[pl.BlockSpec(memory_space=pl.ANY)] * len(arrays),
+        scratch_shapes=[pltpu.SemaphoreType.DMA((len(arrays),))],
+        compiler_params=pltpu.CompilerParams(vmem_limit_bytes=60 * 2**20),
+    )(*arrays)
 
 
 def on_device(n, *args):
@@ -496,45 +532,45 @@
     _, slots, layers, cells = pressure.shape
     quarter = cells // 4
     wide = cells + 2 * HALO
-    table = jnp.concatenate([neighbors[0], tiles[0][:, None], atm_map[0]], axis=1)
-    table = jnp.pad(table, ((0, 0), (0, STRIDE - table.shape[1]))).reshape(1, slots * STRIDE)
-    table = jnp.pad(table, ((0, 0), (0, -table.shape[1] % LANES)))
-    width = table.shape[1]
+    elev, land, rain = (jnp.transpose(v, (1, 0, 2)) for v in (elev, land, rain))
+    neighbors, atm_map = (jnp.transpose(v, (0, 2, 1)) for v in (neighbors, atm_map))
     vec, smem, anywhere = pltpu.VMEM, pltpu.SMEM, pl.ANY
 
     def cube(kind=jnp.float32):
         return vec((slots, layers, wide), kind)
 
-    def flat(kind=jnp.float32):
-        return vec((slots, wide), kind)
-
     def lines(kind=jnp.float32):
         return vec((slots, 1, wide), kind)
 
     dma = pltpu.SemaphoreType.DMA
-    return tuple(pl.pallas_call(
+    made = pl.pallas_call(
         functools.partial(kernel, n),
         out_shape=[
             jax.ShapeDtypeStruct(pressure.shape, jnp.float32),
             jax.ShapeDtypeStruct((1, slots, 4, quarter), jnp.float32),
         ],
-        in_specs=[pl.BlockSpec(memory_space=anywhere)] * 7
-        + [pl.BlockSpec(memory_space=smem), pl.BlockSpec(memory_space=vec)],
-        out_specs=[pl.BlockSpec(memory_space=anywhere), pl.BlockSpec(memory_space=vec)],
+        in_specs=[pl.BlockSpec(memory_space=anywhere)] * 10,
+        out_specs=[pl.BlockSpec(memory_space=anywhere)] * 2,
         scratch_shapes=[
             cube(),
             cube(),
             cube(jnp.int32),
-            flat(),
-            flat(jnp.int32),
-            flat(),
             lines(),
             lines(jnp.int32),
             lines(),
-            vec((1, width), jnp.int32),
-            vec((1, width), jnp.int32),
-            smem((1, width), jnp.int32),
-            smem((1, width), jnp.int32),
+            vec((1, 4, slots), jnp.int32),
+            vec((1, 4, slots), jnp.int32),
+            vec((1, slots), jnp.int32),
+            vec((1, slots), jnp.int32),
+            smem((1, 4, slots), jnp.int32),
+            smem((1, 4, slots), jnp.int32),
+            smem((1, slots), jnp.int32),
+            smem((1, slots), jnp.int32),
+            smem((1, 4, slots), jnp.int32),
+            smem((1, slots), jnp.int32),
+            smem((1, 4, slots), jnp.int32),
+            vec(forcing.shape, jnp.float32),
+            vec((1, slots, 4, quarter), jnp.float32),
         ]
         + [cube()] * 20
         + [
@@ -544,20 +580,21 @@
             vec((n, 1, quarter + LANES), jnp.float32),
             vec((n, 1, quarter), jnp.float32),
             vec((n, 1, quarter), jnp.float32),
-            dma((6,)),
-            dma((2, 7)),
-            dma((2, 7)),
+            dma((10,)),
+            dma((2, 8)),
+            dma((2, 8)),
+            dma((4,)),
+            dma,
+            dma,
+            dma,
+            dma,
             dma((2,)),
-            dma((n,)),
-            dma((n,)),
-            dma((n,)),
-            dma((n,)),
-            dma,
         ],
         compiler_params=pltpu.CompilerParams(
             collective_id=0, has_side_effects=True, vmem_limit_bytes=60 * 2**20
         ),
-    )(pressure, pressure_old, soil, elev, land, rain, table, table, forcing))
+    )(pressure, pressure_old, soil, elev, land, rain, neighbors, tiles, atm_map, forcing)
+    return tuple(hand_over(made))
 
 
 def solution(mesh):

time: 41.6 us -> 41.1 us (0.988)
  Pallas kernels: 34.8 us -> 40.3 us
  local copies, waits for them, and re-layouts: 5.03 us -> 0 us
  other arithmetic: 0.73 us -> 0 us
    pallas_call x0 -> x1, Pallas kernels: none -> 7.82 us  [hand_over(): pl.pallas_call(copy_kernel, out_shape=[jax.ShapeDtypeStruct(v.shape, v.dt...]
    unnamed x14 -> x0, local copies, waits for them, and re-layouts: 4.43 us -> none
    pallas_call x1, Pallas kernels: 34.8 us -> 32.5 us  [on_device(): pl.pallas_call(functools.partial(kernel, n), out_shape=[jax.ShapeDtypeStr...]
    concatenate x1 -> x0, other arithmetic: 0.73 us -> none  [on_device(): jnp.concatenate([neighbors[0], tiles[0][:, None], atm_map[0]], axis=1)]
    pad x2 -> x0, local copies, waits for them, and re-layouts: 0.53 us -> none  [the longest x1 0.52 us: on_device(): table = jnp.pad(table, ((0, 0), (0, -table.shape[1] % LANES)))]
where the time goes in v1:
time: 41.1 us; the launch traced here: 41 us
  Pallas kernels  40.3 us (98%)
  between operations  0.64 us (2%)
    pallas_call x1, Pallas kernels, on_device(): pl.pallas_call(functools.partial(kernel, n), out_shape=[jax.ShapeDtypeStr...  32.5 us
    pallas_call x1, Pallas kernels, hand_over(): pl.pallas_call(copy_kernel, out_shape=[jax.ShapeDtypeStruct(v.shape, v.dt...  7.82 us

profile of v1, /device:TPU:0, one launch (start us, length us, event | category | flops | bytes accessed | tf_op | source)
XLA Modules:
  0.0 41.0 jit_solution(1196115029860259080)
XLA Ops:
  0.6 32.5 %shard_map.113 = (f32[1,6,8,1024]{3,2,1,0:T(8,128)}, f32[1,6,4,256]{3,2,1,0:T(4,128)}) custom-call(f32[1,6,8,1024]{3,2,1,0:T(8,128)} %p_in.1, f32[1,6,8,1024]{3,2,1,0:T(8,128)} %old_in.1, s32[1,6,8,1024]{3,2,1,0:T(8,128)} %soil_in.1, f32[6,1,1024]{2,1,0:T(1,128)} %bitcast.5, s32[6,1,1024]{2,1,0:T(1,128)} %bitcast.6, f32[6,1,1024]{2,1,0:T(1,128)} %bitcast.7, ...), custom_call_target="tpu_custom_call" | custom-call | tf_op jit(solution)/shard_map/pallas_call | solution.py:546
  33.2 7.8 %shard_map.114 = (f32[1,6,8,1024]{3,2,1,0:T(8,128)}, f32[1,6,4,256]{3,2,1,0:T(4,128)}) custom-call(f32[1,6,8,1024]{3,2,1,0:T(8,128)} %get-tuple-element.4.refs_0_, f32[1,6,4,256]{3,2,1,0:T(4,128)} %get-tuple-element.5.refs_1_), custom_call_target="tpu_custom_call" | custom-call | tf_op jit(solution)/shard_map/pallas_call | solution.py:520

commit v2 on v1

--- a/solution.py
+++ b/solution.py
@@ -25,8 +25,9 @@
 MESH = pl.DeviceIdType.MESH
 
 
-def sigmoid(v):
-    return 1.0 / (1.0 + jnp.exp(-v))
+def inverse(v):
+    guess = pl.reciprocal(v, approx=True)
+    return guess * (2.0 - v * guess)
 
 
 def kernel(
@@ -42,6 +43,7 @@
     atm_in,
     forcing_in,
     p_out,
+    added_out,
     ret_out,
     h,
     cst,
@@ -62,6 +64,7 @@
     own_atm,
     forcing,
     ret,
+    added,
     kk,
     kp,
     hh,
@@ -138,7 +141,7 @@
         )
         return carry
 
-    lax.fori_loop(1, n, greet, 0)
+    lax.fori_loop(1, n, greet, 0, unroll=n <= 32)
     pl.semaphore_wait(barrier, n - 1)
 
     def halo_copies(way):
@@ -195,9 +198,11 @@
     def tile(q, s):
         return (north_tile if q < hc else (own_tile if q < nq - hc else south_tile))[0, s]
 
-    def picks(s, first, last):
+    def picks(s, parts):
         found = {}
         for sec, q in ((0, 0), (1, hc), (2, nq - hc)):
+            if all(section(part) != sec for part in parts):
+                continue
             side = []
             for f in range(4):
                 number = neighbor(q, s, f)
@@ -230,10 +235,10 @@
         return mid, west, east, north, south
 
     def conductivity(s, q, head):
-        relative = sigmoid(2.0 * head)
-        conduct = sat[s, :, at(q)] * relative
+        bend = jnp.tanh(head)
+        conduct = sat[s, :, at(q)] * (1.0 + bend)
         kk[s, :, at(q)] = conduct
-        kp[s, :, at(q)] = 2.0 * conduct * (1.0 - relative)
+        kp[s, :, at(q)] = conduct * (1.0 - bend)
 
     def prepare(parts, s, carry):
         for q in parts:
@@ -245,12 +250,13 @@
                     jnp.where(hit, float(t[number]), v)
                     for t, v in zip((KSAT, SHAPE, POROSITY), tables)
                 ]
-            sat[s, :, at(q)] = 0.5 * tables[0]
-            alpha[s, :, at(q)] = tables[1]
-            poro[s, :, at(q)] = tables[2]
+            sat[s, :, at(q)] = 0.25 * tables[0]
+            half_shape, eighth = 0.5 * tables[1], 0.125 * tables[2]
+            alpha[s, :, at(q)] = half_shape
+            poro[s, :, at(q)] = eighth
             old = cst[s, :, at(q)]
             rain_top = jnp.where(layer == 0, rain[s, :, at(q)], 0.0)
-            cst[s, :, at(q)] = 0.25 * (old + tables[2] * sigmoid(tables[1] * old)) + rain_top
+            cst[s, :, at(q)] = 0.25 * old + eighth * jnp.tanh(half_shape * old) + rain_top
             held = jnp.where(tile(q, s) >= 0, 1.0, 0.0)
             wet[s, :, at(q)] = jnp.broadcast_to(
                 jnp.where(land[s, :, at(q)] > 0, held, 0.0), (layers, LANES)
@@ -260,40 +266,9 @@
             conductivity(s, q, head)
         return carry
 
-    lax.fori_loop(0, slots, functools.partial(prepare, range(hc, nq - hc)), 0)
-
-    @pl.when(me > 0)
-    def _():
-        for copy in halo_copies(0):
-            copy.wait_recv()
-
-    @pl.when(me < n - 1)
-    def _():
-        for copy in halo_copies(1):
-            copy.wait_recv()
-
-    tabs = [
-        pltpu.make_async_copy(src, dst, tab_sem.at[i])
-        for i, (src, dst) in enumerate(
-            (
-                (north_nb_vec, north_nb),
-                (south_nb_vec, south_nb),
-                (north_tile_vec, north_tile),
-                (south_tile_vec, south_tile),
-            )
-        )
-    ]
-    for copy in tabs:
-        copy.start()
-    for copy in tabs:
-        copy.wait()
-
-    halo_parts = tuple(range(hc)) + tuple(range(nq - hc, nq))
-    lax.fori_loop(0, slots, functools.partial(prepare, halo_parts), 0)
-
-    def balance(first, last, s, carry):
-        found = picks(s, first, last)
-        for q in range(first, last):
+    def balance(parts, s, carry):
+        found = picks(s, parts)
+        for q in parts:
             side = found[section(q)]
             k0, k_w, k_e, k_n, k_s = around(kk, s, q, found)
             h0, h_w, h_e, h_n, h_s = around(hh, s, q, found)
@@ -334,19 +309,19 @@
             head = h[s, :, at(q)]
             shape = alpha[s, :, at(q)]
             pore = poro[s, :, at(q)]
-            theta = sigmoid(shape * head)
-            storage = 0.25 * (1.0 + pore * shape * theta * (1.0 - theta))
-            residual = 0.25 * (head + pore * theta) - cst[s, :, at(q)] - inflow
-            scaled = wet[s, :, at(q)] / (storage + total)
+            bend = jnp.tanh(shape * head)
+            storage = 0.25 + pore * shape * (1.0 - bend * bend)
+            residual = 0.25 * head + pore * bend - cst[s, :, at(q)] - inflow
+            scaled = wet[s, :, at(q)] * inverse(storage + total)
             move = scaled * residual
             wi[s, :, at(q)] = scaled
             step[s, :, at(q)] = move
             qq[s, :, at(q)] = kp[s, :, at(q)] * move
         return carry
 
-    def advance(first, last, final, s, carry):
-        found = picks(s, first, last)
-        for q in range(first, last):
+    def advance(parts, final, s, carry):
+        found = picks(s, parts)
+        for q in parts:
             s0, s_w, s_e, s_n, s_s = around(step, s, q, found)
             q0, q_w, q_e, q_n, q_s = around(qq, s, q, found)
             gsum = acc = None
@@ -368,7 +343,7 @@
             head = h[s, :, at(q)] - change
             h[s, :, at(q)] = head
             if final:
-                strength = 2.0 * wet[s, :, at(q)] * sat[s, :, at(q)] * sigmoid(2.0 * head)
+                strength = 2.0 * wet[s, :, at(q)] * (sat[s, :, at(q)] * (1.0 + jnp.tanh(head)))
                 half, part = divmod(q - hc, HALO // LANES)
                 flux[s * 4 + half, :, pl.ds(part * LANES, LANES)] = strength[0:1]
             else:
@@ -376,46 +351,83 @@
                 conductivity(s, q, head)
         return carry
 
+    lax.fori_loop(0, slots, functools.partial(prepare, range(hc, nq - hc)), 0)
+    inner = tuple(range(hc + 1, nq - hc - 1))
+    lax.fori_loop(0, slots, functools.partial(balance, inner), 0)
+
+    quarter = flux.shape[-1]
+    place = lax.broadcasted_iota(jnp.int32, (n, LANES), 0) * atm
+
+    def name(s, label):
+        for k in range(4):
+            there = own_atm[0, k, s] - place
+            hit = (there >= 0) & (there < atm)
+            label = jnp.where(hit, (there + 1).astype(jnp.float32), label)
+        return label
+
+    label = lax.fori_loop(0, slots, name, jnp.zeros((n, LANES), jnp.float32))
+    for d in range(n):
+        snd[d, :, pl.ds(quarter, LANES)] = label[d : d + 1]
+
+    @pl.when(me > 0)
+    def _():
+        for copy in halo_copies(0):
+            copy.wait_recv()
+
+    @pl.when(me < n - 1)
+    def _():
+        for copy in halo_copies(1):
+            copy.wait_recv()
+
+    tabs = [
+        pltpu.make_async_copy(src, dst, tab_sem.at[i])
+        for i, (src, dst) in enumerate(
+            (
+                (north_nb_vec, north_nb),
+                (south_nb_vec, south_nb),
+                (north_tile_vec, north_tile),
+                (south_tile_vec, south_tile),
+            )
+        )
+    ]
+    for copy in tabs:
+        copy.start()
+    for copy in tabs:
+        copy.wait()
+
+    halo_parts = tuple(range(hc)) + tuple(range(nq - hc, nq))
+    lax.fori_loop(0, slots, functools.partial(prepare, halo_parts), 0)
+
+
     rows_per = LANES // TS
     for number in range(ITERS):
         rows_a = 2 * ITERS - 1 - 2 * number
         rows_b = rows_a - 1
         wide_a, wide_b = -(-rows_a // rows_per), -(-rows_b // rows_per)
+        parts_a = range(hc - wide_a, nq - hc + wide_a)
+        if number == 0:
+            parts_a = tuple(q for q in parts_a if q not in inner)
+        parts_b = range(hc - wide_b, nq - hc + wide_b)
+        lax.fori_loop(0, slots, functools.partial(balance, parts_a), 0)
         lax.fori_loop(
-            0, slots, functools.partial(balance, hc - wide_a, nq - hc + wide_a), 0
+            0, slots, functools.partial(advance, parts_b, number == ITERS - 1), 0
         )
-        lax.fori_loop(
-            0,
-            slots,
-            functools.partial(advance, hc - wide_b, nq - hc + wide_b, number == ITERS - 1),
-            0,
-        )
-
-    quarter = flux.shape[-1]
-    place = lax.broadcasted_iota(jnp.int32, (n, LANES), 0) * atm
+
+    head_out = pltpu.make_async_copy(h.at[:, :, own], p_out.at[0], out_sem.at[0])
+    head_out.start()
+
     wide_place = lax.broadcasted_iota(jnp.int32, (n, quarter), 0) * atm
 
-    def collect(s, carry):
-        sums, label = carry
+    def collect(s, sums):
         for k in range(4):
-            number = own_atm[0, k, s]
-            there = number - wide_place
+            there = own_atm[0, k, s] - wide_place
             hit = (there >= 0) & (there < atm)
             sums = sums + jnp.where(hit, flux[s * 4 + k], 0.0)
-            there = number - place
-            hit = (there >= 0) & (there < atm)
-            label = jnp.where(hit, (there + 1).astype(jnp.float32), label)
-        return sums, label
-
-    sums, label = lax.fori_loop(
-        0,
-        slots,
-        collect,
-        (jnp.zeros((n, quarter), jnp.float32), jnp.zeros((n, LANES), jnp.float32)),
-    )
+        return sums
+
+    sums = lax.fori_loop(0, slots, collect, jnp.zeros((n, quarter), jnp.float32))
     for d in range(n):
         snd[d, :, pl.ds(0, quarter)] = sums[d : d + 1]
-        snd[d, :, pl.ds(quarter, LANES)] = label[d : d + 1]
 
     def exchange(src, dst, s_sem, r_sem):
         def one(o):
@@ -433,7 +445,7 @@
             one(o).start()
             return carry
 
-        lax.fori_loop(1, n, begin, 0)
+        lax.fori_loop(1, n, begin, 0, unroll=n <= 32)
         dst[me] = src[me]
         everyone = pltpu.make_async_copy(
             src.at[pl.ds(0, n - 1)], dst.at[pl.ds(0, n - 1)], r_sem
@@ -473,17 +485,15 @@
             rate = rcv2[lax.div(jnp.maximum(number, 0), atm)] * live
             ret[0, s, pl.ds(k, 1), :] = rate
             for part in range(quarter // LANES):
-                q = hc + k * (quarter // LANES) + part
+                q = k * (quarter // LANES) + part
                 piece = rate[:, part * LANES : (part + 1) * LANES]
-                h[s, :, at(q)] = h[s, :, at(q)] + jnp.where(
-                    layer == 0, COUPLING * wet[s, :, at(q)] * piece, 0.0
-                )
+                added[s, :, at(q)] = COUPLING * wet[s, 0:1, at(hc + q)] * piece
         return carry
 
     lax.fori_loop(0, slots, settle, 0)
     outs = [
-        pltpu.make_async_copy(h.at[:, :, own], p_out.at[0], out_sem.at[0]),
-        pltpu.make_async_copy(ret, ret_out, out_sem.at[1]),
+        pltpu.make_async_copy(added, added_out, out_sem.at[1]),
+        pltpu.make_async_copy(ret, ret_out, out_sem.at[2]),
     ]
     for copy in outs:
         copy.start()
@@ -500,31 +510,59 @@
         for copy in halo_copies(1):
             copy.wait_send()
 
+    head_out.wait()
     for copy in outs:
         copy.wait()
 
 
-def copy_kernel(*refs):
-    count = len(refs) // 2
-    sems = refs[-1]
-    copies = [
-        pltpu.make_async_copy(refs[i], refs[count + i], sems.at[i]) for i in range(count)
+def couple_kernel(
+    head_in, added_in, rate_in, head_out, rate_out, head, added, rate, in_sem, out_sem, side_sem
+):
+    slots = head.shape[0]
+    loads = [
+        pltpu.make_async_copy(head_in.at[0, s], head.at[s], in_sem.at[s]) for s in range(slots)
     ]
-    for copy in copies:
+    stores = [
+        pltpu.make_async_copy(head.at[s], head_out.at[0, s], out_sem.at[s]) for s in range(slots)
+    ]
+    load_added = pltpu.make_async_copy(added_in, added, side_sem.at[0])
+    load_rate = pltpu.make_async_copy(rate_in, rate, side_sem.at[1])
+    store_rate = pltpu.make_async_copy(rate, rate_out, side_sem.at[2])
+    load_added.start()
+    for copy in loads:
         copy.start()
-    for copy in copies:
+    load_rate.start()
+    load_added.wait()
+    for s in range(slots):
+        loads[s].wait()
+        head[s, 0:1, :] = head[s, 0:1, :] + added[s]
+        stores[s].start()
+    load_rate.wait()
+    store_rate.start()
+    for copy in stores:
         copy.wait()
-
-
-def hand_over(arrays):
+    store_rate.wait()
+
+
+def couple(head, added, rate):
+    dma = pltpu.SemaphoreType.DMA
+    slots = head.shape[1]
+    anywhere = pl.BlockSpec(memory_space=pl.ANY)
     return pl.pallas_call(
-        copy_kernel,
-        out_shape=[jax.ShapeDtypeStruct(v.shape, v.dtype) for v in arrays],
-        in_specs=[pl.BlockSpec(memory_space=pl.ANY)] * len(arrays),
-        out_specs=[pl.BlockSpec(memory_space=pl.ANY)] * len(arrays),
-        scratch_shapes=[pltpu.SemaphoreType.DMA((len(arrays),))],
+        couple_kernel,
+        out_shape=[jax.ShapeDtypeStruct(v.shape, v.dtype) for v in (head, rate)],
+        in_specs=[anywhere] * 3,
+        out_specs=[anywhere] * 2,
+        scratch_shapes=[
+            pltpu.VMEM(head.shape[1:], head.dtype),
+            pltpu.VMEM(added.shape, added.dtype),
+            pltpu.VMEM(rate.shape, rate.dtype),
+            dma((slots,)),
+            dma((slots,)),
+            dma((3,)),
+        ],
         compiler_params=pltpu.CompilerParams(vmem_limit_bytes=60 * 2**20),
-    )(*arrays)
+    )(head, added, rate)
 
 
 def on_device(n, *args):
@@ -547,10 +585,11 @@
         functools.partial(kernel, n),
         out_shape=[
             jax.ShapeDtypeStruct(pressure.shape, jnp.float32),
+            jax.ShapeDtypeStruct((slots, 1, cells), jnp.float32),
             jax.ShapeDtypeStruct((1, slots, 4, quarter), jnp.float32),
         ],
         in_specs=[pl.BlockSpec(memory_space=anywhere)] * 10,
-        out_specs=[pl.BlockSpec(memory_space=anywhere)] * 2,
+        out_specs=[pl.BlockSpec(memory_space=anywhere)] * 3,
         scratch_shapes=[
             cube(),
             cube(),
@@ -571,6 +610,7 @@
             smem((1, 4, slots), jnp.int32),
             vec(forcing.shape, jnp.float32),
             vec((1, slots, 4, quarter), jnp.float32),
+            vec((slots, 1, cells), jnp.float32),
         ]
         + [cube()] * 20
         + [
@@ -588,13 +628,13 @@
             dma,
             dma,
             dma,
-            dma((2,)),
+            dma((3,)),
         ],
         compiler_params=pltpu.CompilerParams(
             collective_id=0, has_side_effects=True, vmem_limit_bytes=60 * 2**20
         ),
     )(pressure, pressure_old, soil, elev, land, rain, neighbors, tiles, atm_map, forcing)
-    return tuple(hand_over(made))
+    return tuple(couple(*made))
 
 
 def solution(mesh):

time: 41.1 us -> 34.2 us (0.83)
  Pallas kernels: 40.3 us -> 33.4 us
    pallas_call x1, Pallas kernels: 7.82 us -> 1.61 us  [couple(): pl.pallas_call(couple_kernel, out_shape=[jax.ShapeDtypeStruct(v.shape, v....]
    pallas_call x1, Pallas kernels: 32.5 us -> 31.8 us  [on_device(): pl.pallas_call(functools.partial(kernel, n), out_shape=[jax.ShapeDtypeStr...]
where the time goes in v2:
time: 34.2 us; the launch traced here: 34.1 us
  Pallas kernels  33.4 us (98%)
  between operations  0.64 us (2%)
    pallas_call x1, Pallas kernels, on_device(): pl.pallas_call(functools.partial(kernel, n), out_shape=[jax.ShapeDtypeStr...  31.8 us
    pallas_call x1, Pallas kernels, couple(): pl.pallas_call(couple_kernel, out_shape=[jax.ShapeDtypeStruct(v.shape, v....  1.61 us

profile of v2, /device:TPU:0, one launch (start us, length us, event | category | flops | bytes accessed | tf_op | source)
XLA Modules:
  0.0 34.1 jit_solution(3251261095736592237)
XLA Ops:
  0.6 31.8 %shard_map.113 = (f32[1,6,8,1024]{3,2,1,0:T(8,128)}, f32[6,1,1024]{2,1,0:T(1,128)}, f32[1,6,4,256]{3,2,1,0:T(4,128)}) custom-call(f32[1,6,8,1024]{3,2,1,0:T(8,128)} %p_in.1, f32[1,6,8,1024]{3,2,1,0:T(8,128)} %old_in.1, s32[1,6,8,1024]{3,2,1,0:T(8,128)} %soil_in.1, f32[6,1,1024]{2,1,0:T(1,128)} %bitcast.5, s32[6,1,1024]{2,1,0:T(1,128)} %bitcast.6, ...), custom_call_target="tpu_custom_call" | custom-call | tf_op jit(solution)/shard_map/pallas_call | solution.py:584
  32.4 1.6 %shard_map.114 = (f32[1,6,8,1024]{3,2,1,0:T(8,128)}, f32[1,6,4,256]{3,2,1,0:T(4,128)}) custom-call(f32[1,6,8,1024]{3,2,1,0:T(8,128)} %get-tuple-element.5.head_in, f32[6,1,1024]{2,1,0:T(1,128)} %get-tuple-element.6.added_in, f32[1,6,4,256]{3,2,1,0:T(4,128)} %get-tuple-element.7.rate_in), custom_call_target="tpu_custom_call" | custom-call | tf_op jit(solution)/shard_map/pallas_call | solution.py:551

commit v3 on v2

--- a/solution.py
+++ b/solution.py
@@ -9,6 +9,7 @@
 from jax.sharding import PartitionSpec as P
 
 TS = 32
+LAG_PREPARE, LAG_BALANCE, LAG_ADVANCE = 3, 2, 3
 ITERS = 4
 LANES = 128
 HALO = 2 * ITERS * TS
@@ -23,6 +24,28 @@
 LAYER_DROP = 0.25
 COUPLING = 0.5
 MESH = pl.DeviceIdType.MESH
+
+
+class Later:
+    def __init__(self, lag):
+        self.lag, self.held, self.now = lag, [], []
+
+    def put(self, ref, place, value):
+        self.now.append((ref, place, value))
+
+    def close(self):
+        self.held.append(self.now)
+        self.now = []
+        if len(self.held) > self.lag:
+            self.write(self.held.pop(0))
+
+    def write(self, stores):
+        for ref, place, value in stores:
+            ref[place] = value
+
+    def flush(self):
+        for stores in self.held:
+            self.write(stores)
 
 
 def inverse(v):
@@ -234,13 +257,14 @@
         south = pltpu.roll(jnp.where(at_north, below, mid), LANES - TS, 1)
         return mid, west, east, north, south
 
-    def conductivity(s, q, head):
+    def conductivity(later, s, q, head, quarter_sat):
         bend = jnp.tanh(head)
-        conduct = sat[s, :, at(q)] * (1.0 + bend)
-        kk[s, :, at(q)] = conduct
-        kp[s, :, at(q)] = conduct * (1.0 - bend)
+        conduct = quarter_sat * (1.0 + bend)
+        later.put(kk, (s, slice(None), at(q)), conduct)
+        later.put(kp, (s, slice(None), at(q)), conduct * (1.0 - bend))
 
     def prepare(parts, s, carry):
+        later = Later(LAG_PREPARE)
         for q in parts:
             classes = soil[s, :, at(q)]
             tables = [jnp.full((layers, LANES), float(t[0]), jnp.float32) for t in (KSAT, SHAPE, POROSITY)]
@@ -250,23 +274,26 @@
                     jnp.where(hit, float(t[number]), v)
                     for t, v in zip((KSAT, SHAPE, POROSITY), tables)
                 ]
-            sat[s, :, at(q)] = 0.25 * tables[0]
+            quarter_sat = 0.25 * tables[0]
+            later.put(sat, (s, slice(None), at(q)), quarter_sat)
             half_shape, eighth = 0.5 * tables[1], 0.125 * tables[2]
-            alpha[s, :, at(q)] = half_shape
-            poro[s, :, at(q)] = eighth
+            later.put(alpha, (s, slice(None), at(q)), half_shape)
+            later.put(poro, (s, slice(None), at(q)), eighth)
             old = cst[s, :, at(q)]
             rain_top = jnp.where(layer == 0, rain[s, :, at(q)], 0.0)
-            cst[s, :, at(q)] = 0.25 * old + eighth * jnp.tanh(half_shape * old) + rain_top
+            later.put(cst, (s, slice(None), at(q)), 0.25 * old + eighth * jnp.tanh(half_shape * old) + rain_top)
             held = jnp.where(tile(q, s) >= 0, 1.0, 0.0)
-            wet[s, :, at(q)] = jnp.broadcast_to(
-                jnp.where(land[s, :, at(q)] > 0, held, 0.0), (layers, LANES)
-            )
+            damp = jnp.where(land[s, :, at(q)] > 0, held, 0.0)
+            later.put(wet, (s, slice(None), at(q)), jnp.broadcast_to(damp, (layers, LANES)))
             head = h[s, :, at(q)]
-            hh[s, :, at(q)] = head + (elev[s, :, at(q)] - depth)
-            conductivity(s, q, head)
+            later.put(hh, (s, slice(None), at(q)), head + (elev[s, :, at(q)] - depth))
+            conductivity(later, s, q, head, quarter_sat)
+            later.close()
+        later.flush()
         return carry
 
     def balance(parts, s, carry):
+        later = Later(LAG_BALANCE)
         found = picks(s, parts)
         for q in parts:
             side = found[section(q)]
@@ -294,15 +321,15 @@
                 weighted = drop
                 if mask is not None:
                     face, weighted = face * mask, drop * mask
-                k_ref[s, :, at(q)] = face
-                g_ref[s, :, at(q)] = weighted
+                later.put(k_ref, (s, slice(None), at(q)), face)
+                later.put(g_ref, (s, slice(None), at(q)), weighted)
                 flow = face * drop
                 inflow = flow if inflow is None else inflow + flow
                 total = face if k_ref is kf_w else total + face
             drop = pltpu.roll(h0, 1, 0) - h0
             face = (k0 + pltpu.roll(k0, 1, 0)) * upper
-            kf_u[s, :, at(q)] = face
-            g_u[s, :, at(q)] = drop * upper
+            later.put(kf_u, (s, slice(None), at(q)), face)
+            later.put(g_u, (s, slice(None), at(q)), drop * upper)
             flow = face * drop
             inflow = inflow + flow - pltpu.roll(flow, layers - 1, 0)
             total = total + face + pltpu.roll(face, layers - 1, 0)
@@ -314,12 +341,15 @@
             residual = 0.25 * head + pore * bend - cst[s, :, at(q)] - inflow
             scaled = wet[s, :, at(q)] * inverse(storage + total)
             move = scaled * residual
-            wi[s, :, at(q)] = scaled
-            step[s, :, at(q)] = move
-            qq[s, :, at(q)] = kp[s, :, at(q)] * move
+            later.put(wi, (s, slice(None), at(q)), scaled)
+            later.put(step, (s, slice(None), at(q)), move)
+            later.put(qq, (s, slice(None), at(q)), kp[s, :, at(q)] * move)
+            later.close()
+        later.flush()
         return carry
 
     def advance(parts, final, s, carry):
+        later = Later(LAG_ADVANCE)
         found = picks(s, parts)
         for q in parts:
             s0, s_w, s_e, s_n, s_s = around(step, s, q, found)
@@ -341,14 +371,18 @@
             gsum = gsum + grad - pltpu.roll(grad, layers - 1, 0)
             change = s0 + wi[s, :, at(q)] * (acc + q0 * gsum)
             head = h[s, :, at(q)] - change
-            h[s, :, at(q)] = head
+            later.put(h, (s, slice(None), at(q)), head)
             if final:
                 strength = 2.0 * wet[s, :, at(q)] * (sat[s, :, at(q)] * (1.0 + jnp.tanh(head)))
                 half, part = divmod(q - hc, HALO // LANES)
-                flux[s * 4 + half, :, pl.ds(part * LANES, LANES)] = strength[0:1]
+                later.put(
+                    flux, (s * 4 + half, slice(None), pl.ds(part * LANES, LANES)), strength[0:1]
+                )
             else:
-                hh[s, :, at(q)] = hh[s, :, at(q)] - change
-                conductivity(s, q, head)
+                later.put(hh, (s, slice(None), at(q)), hh[s, :, at(q)] - change)
+                conductivity(later, s, q, head, sat[s, :, at(q)])
+            later.close()
+        later.flush()
         return carry
 
     lax.fori_loop(0, slots, functools.partial(prepare, range(hc, nq - hc)), 0)

time: 34.2 us -> 34.2 us (level)
  no operation moved by 1% of the time
where the time goes in v3:
time: 34.2 us; the launch traced here: 34.1 us
  Pallas kernels  33.4 us (98%)
  between operations  0.64 us (2%)
    pallas_call x1, Pallas kernels, on_device(): pl.pallas_call(functools.partial(kernel, n), out_shape=[jax.ShapeDtypeStr...  31.8 us
    pallas_call x1, Pallas kernels, couple(): pl.pallas_call(couple_kernel, out_shape=[jax.ShapeDtypeStruct(v.shape, v....  1.61 us

profile of v3, /device:TPU:0, one launch (start us, length us, event | category | flops | bytes accessed | tf_op | source)
XLA Modules:
  0.0 34.1 jit_solution(13661561866658218551)
XLA Ops:
  0.6 31.8 %shard_map.113 = (f32[1,6,8,1024]{3,2,1,0:T(8,128)}, f32[6,1,1024]{2,1,0:T(1,128)}, f32[1,6,4,256]{3,2,1,0:T(4,128)}) custom-call(f32[1,6,8,1024]{3,2,1,0:T(8,128)} %p_in.1, f32[1,6,8,1024]{3,2,1,0:T(8,128)} %old_in.1, s32[1,6,8,1024]{3,2,1,0:T(8,128)} %soil_in.1, f32[6,1,1024]{2,1,0:T(1,128)} %bitcast.5, s32[6,1,1024]{2,1,0:T(1,128)} %bitcast.6, ...), custom_call_target="tpu_custom_call" | custom-call | tf_op jit(solution)/shard_map/pallas_call | solution.py:618
  32.4 1.6 %shard_map.114 = (f32[1,6,8,1024]{3,2,1,0:T(8,128)}, f32[1,6,4,256]{3,2,1,0:T(4,128)}) custom-call(f32[1,6,8,1024]{3,2,1,0:T(8,128)} %get-tuple-element.5.head_in, f32[6,1,1024]{2,1,0:T(1,128)} %get-tuple-element.6.added_in, f32[1,6,4,256]{3,2,1,0:T(4,128)} %get-tuple-element.7.rate_in), custom_call_target="tpu_custom_call" | custom-call | tf_op jit(solution)/shard_map/pallas_call | solution.py:585
